TPU v7x, 512 devices: a whole 4x8x8 slice. The times are simulated.
512 devices in a mesh: grp: 16 (over x, y_lo), cell: 32 (over z, y_hi, core).
Axes of the slice: x: 4, y: 8 (y_hi: 2, y_lo: 4; y = y_hi * 4 + y_lo), z: 8, core: 2. Of those that a mesh axis runs over, the one named last changes fastest.
Arguments:
- snapshots: bfloat16 [98304, 2048], P('cell', 'grp'), may hold values from -40 to 40
- density: float32 [8], replicated, may hold values from 0.25 to 4
Outputs:
- gram: float32 [2048, 2048], P('grp', 'cell')
All inputs are finite; a program needn't handle non-finite values.
Results may differ from a plain program's by a relative error of at most 0.00074.
Values may be sent and summed in bfloat16 or wider, within the bound.
A program may use at most 64 MiB of HBM per device.

v0:
```python
import jax
import jax.numpy as jnp
from jax import lax
from jax.sharding import PartitionSpec as P

REG = 8


def pair_tile(left, right):
    return jnp.einsum("ca,cb->ab", left, right, preferred_element_type=jnp.float32)


def body(snapshots, density):
    cell_count, group_width = snapshots.shape
    slab_count = lax.axis_size("cell")
    total_cells = cell_count * slab_count
    positions = lax.axis_index("cell") * cell_count + lax.iota(jnp.int32, cell_count)
    zones = positions * REG // total_cells
    matches = zones[:, None] == lax.iota(jnp.int32, REG)[None, :]
    chosen = jnp.sum(jnp.where(matches, density[None, :], 0.0), axis=1)
    weighted = (snapshots.astype(jnp.float32) * jnp.sqrt(chosen)[:, None]).astype(jnp.bfloat16)
    partial_row = pair_tile(weighted, lax.all_gather(weighted, "grp", axis=1, tiled=True))
    summed = lax.psum_scatter(partial_row, "cell", scatter_dimension=1, tiled=True)
    return summed / total_cells


def solution(mesh):
    in_specs = (P("cell", "grp"), P())
    out_specs = P("grp", "cell")
    return jax.shard_map(body, mesh=mesh, in_specs=in_specs, out_specs=out_specs, check_vma=False)
```

profile of v0, /device:TPU:4, one launch (start us, length us, event | category | flops | bytes accessed | tf_op | source)
XLA Modules:
  0.0 433.4 jit_solution(8274970888036418479)
XLA Ops:
  6.5 0.0 all-gather.2.cloned.1.call-start
  6.6 0.8 select_reduce_fusion
  7.3 2.5 multiply_convert_fusion
  9.8 0.0 all-gather.2.cloned.1.call-update
  9.8 0.0 reduce-scatter.2.cloned.1.call-start
  9.9 276.2 %all-gather.2.cloned.1.call-done = bf16[3072,2048]{1,0:T(8,128)(2,1)} async-done(((bf16[3072,128]{1,0:T(8,128)(2,1)}), bf16[3072,2048]{1,0:T(8,128)(2,1)}) %all-gather.2.cloned.1.call-update) | async-done | bytes 12582928 | tf_op jit(solution)/shard_map/all_gather | solution.py:22
  286.1 10.9 %fusion.1 = f32[128,2048]{0,1:T(8,128)} fusion(bf16[3072,128]{1,0:T(8,128)(2,1)} %multiply_convert_fusion, bf16[3072,2048]{1,0:T(8,128)(2,1)} %all-gather.2.cloned.1.call-done), kind=kOutput, calls=%fused_computation.9 | convolution fusion | flops 1610612736 | bytes 14417920 | tf_op jit(solution)/shard_map/ca,cb->ab/dot_general | solution.py:10
  297.0 0.0 reduce-scatter.2.cloned.1.call-update
  297.0 128.2 %reduce-scatter.2.cloned.1.call-done = f32[128,64]{0,1:T(8,128)} async-done(((f32[128,2048]{0,1:T(8,128)}), f32[128,64]{0,1:T(8,128)}) %reduce-scatter.2.cloned.1.call-update) | async-done | bytes 32784 | tf_op jit(solution)/shard_map/reduce_scatter | solution.py:23
  425.2 1.4 broadcast_multiply_fusion
  (2 shorter events, 0.0 us)
Async XLA Ops:
  6.5 279.6 %all-gather.2.cloned.1.call-start = ((), (), s32[]{:S(2)}) async-start(), calls=%async_computation.1 | async-start | bytes 13369344 | tf_op jit(solution)/shard_map/all_gather | solution.py:22
  9.8 415.3 %reduce-scatter.2.cloned.1.call-start = ((), (), s32[]{:S(2)}) async-start(), calls=%async_computation.2 | async-start | bytes 1081344 | tf_op jit(solution)/shard_map/reduce_scatter | solution.py:23
Sparse Core Ops, SparseCore 0:
  10.0 276.0 all-gather.1
  297.1 128.0 reduce-scatter.1
where the time goes:
time: 434 us; the launch traced here: 433 us
  waiting for transfers between devices  404 us (93%)
  between operations  13.4 us (3%)
  matrix products  10.9 us (3%)
  other arithmetic  4.63 us (1%)
    all_gather x1, waiting for transfers between devices, body(): lax.all_gather(weighted, 'grp', axis=1, tiled=True)  276 us
    reduce_scatter x1, waiting for transfers between devices, body(): lax.psum_scatter(partial_row, 'cell', scatter_dimension=1, tiled=True)  128 us
    dot_general x1, matrix products, pair_tile(): jnp.einsum('ca,cb->ab', left, right, preferred_element_type=jnp.float32)  10.9 us
  transfers between devices with their start and end apart: 2, of which 2 were waited for; matrix products, arithmetic and copies ran while one was open for 0% of the time, Pallas kernels for 0%

commit v1 on v0

v1 whole, which is shorter than its diff:
```python
import jax
import jax.numpy as jnp
from jax import lax
from jax.experimental import pallas as pl
from jax.experimental.pallas import tpu as pltpu
from jax.sharding import PartitionSpec as P

MESH = pl.DeviceIdType.MESH
CELLS = 98304
SLAB = 3072
QUARTER = SLAB // 4
HALF = QUARTER // 2
SNAP = 128


def device(x, y, z, core):
    return x * 4 + y % 4, (z * 2 + y // 4) * 2 + core


def copy_to(src, dst, send, recv, target):
    return pltpu.make_async_remote_copy(
        src_ref=src, dst_ref=dst, send_sem=send, recv_sem=recv, device_id=target, device_id_type=MESH
    )


def kernel(
    snap_hbm, density_ref, out_ref,
    snap, turned, own, next1, next2, part, peer_part, arrived, total, tiles, mine, other,
    load_sem, y_send, y_recv, x1_send, x1_recv, x2_send, x2_recv, core_send, core_recv,
    ring_send, ring_recv, tile_send, tile_recv, last_send, last_recv, plane_sem, all_sem,
):
    grp, cell = lax.axis_index("grp"), lax.axis_index("cell")
    x, ylo, z, core = grp // 4, grp % 4, cell // 4, cell % 2
    y = (cell // 2) % 2 * 4 + ylo
    y_base = y - ylo
    peer = (grp, cell + 1 - 2 * core)

    load = pltpu.make_async_copy(snap_hbm, snap, load_sem)
    load.start()

    barrier = pltpu.get_barrier_semaphore()

    def greet(sem, d, axis):
        target = {
            "x": lambda: device((x + d) % 4, y, z, core),
            "y": lambda: device(x, (y + d) % 8, z, core),
            "z": lambda: device(x, y, (z + d) % 8, core),
        }[axis]()
        pl.semaphore_signal(sem, inc=1, device_id=target, device_id_type=MESH)

    for d in range(1, 4):
        greet(barrier, d, "x")
    for d in range(1, 8):
        greet(barrier, d, "y")
        greet(barrier, d, "z")
    pl.semaphore_signal(barrier, inc=1, device_id=peer, device_id_type=MESH)

    load.wait()
    scale = jnp.sqrt(jnp.full((1, SNAP), density_ref[z], jnp.float32))
    for q in range(4):
        block = snap[pl.ds(q * QUARTER, QUARTER), :].astype(jnp.float32) * scale
        turned[q] = block.astype(jnp.bfloat16).T
    own[ylo] = turned[ylo]
    pl.semaphore_wait(barrier, 18)

    def y_copy(q):
        return copy_to(
            turned.at[q], own.at[ylo], y_send.at[q], y_recv.at[ylo], device(x, y_base + q, z, core)
        )

    def y_arrival(q):
        return copy_to(turned.at[q], own.at[q], y_send.at[q], y_recv.at[q], device(x, y_base + q, z, core))

    def other_y(d):
        return (ylo + d) % 4

    for d in (1, 2, 3):
        y_copy(other_y(d)).start()

    half = x // 2
    half_next2 = ((x + 2) % 4) // 2

    def x1_copy(q):
        return copy_to(
            own.at[q], next1.at[q], x1_send.at[q], x1_recv.at[q], device((x + 3) % 4, y, z, core)
        )

    def x2_copy(q):
        lanes = pl.ds(pl.multiple_of(half_next2 * HALF, HALF), HALF)
        return copy_to(
            own.at[q, :, lanes], next2.at[q], x2_send.at[q], x2_recv.at[q], device((x + 2) % 4, y, z, core)
        )

    x1_copy(ylo).start()
    x2_copy(ylo).start()

    for d in range(1, 8):
        greet(plane_sem, d, "y")

    for d in (1, 2, 3):
        q = other_y(d)
        y_arrival(q).wait_recv()
        x1_copy(q).start()
        x2_copy(q).start()

    pl.semaphore_wait(plane_sem, 7)
    for d in range(1, 4):
        greet(all_sem, d, "x")

    def multiply(g, left, right):
        product = lax.dot_general(
            left, right, (((1,), (1,)), ((), ())), preferred_element_type=jnp.float32
        )
        for n in range(8):
            for h in range(2):
                for t in range(4):
                    part[g, h, t // 2, n, t % 2] = product[
                        n * 64 + h * 32 : n * 64 + h * 32 + 32, t * 128 : t * 128 + 128
                    ]

    def core_copy(g):
        return copy_to(part.at[g, 1 - core], peer_part.at[g], core_send.at[g], core_recv.at[g], peer)

    def ring_copy(g, colour, d):
        if colour == 0:
            here, there = z, (z + d) % 8
            target = device(x, y, there, core)
        else:
            here, there = y, (y + d) % 8
            target = device(x, there, z, core)
        return copy_to(
            part.at[g, core, colour, there],
            arrived.at[g, colour, here],
            ring_send.at[g, colour],
            ring_recv.at[g, colour],
            target,
        )

    def spread(g):
        core_copy(g).wait_recv()
        part[g, core] = part[g, core] + peer_part[g]

        @pl.loop(1, 8)
        def _(d):
            ring_copy(g, 0, d).start()
            ring_copy(g, 1, d).start()

    left = own[...].reshape(512, QUARTER)
    multiply(0, left, left)
    core_copy(0).start()

    for q in range(4):
        x1_copy(q).wait_recv()
    multiply(1, own[...].reshape(512, QUARTER), next1[...].reshape(512, QUARTER))
    core_copy(1).start()
    spread(0)

    for q in range(4):
        x2_copy(q).wait_recv()
    lanes = pl.ds(pl.multiple_of(half * HALF, HALF), HALF)
    multiply(2, own[:, :, lanes].reshape(512, HALF), next2[...].reshape(512, HALF))
    core_copy(2).start()
    spread(1)
    spread(2)
    pl.semaphore_wait(all_sem, 3)

    def tile_copies(g, colour, t, act):
        k = 2 * colour + t
        where, index = (z, y) if colour == 0 else (y, z)
        row = x * 4 + where // 2
        column = ((x + g) % 4) * 4 + k
        targets = [(0, row, 2 * column + core)]
        if g > 0:
            targets.append((1, column, 2 * row + core))
        for kind, to_grp, to_cell in targets:
            here = jnp.logical_and(to_grp == grp, to_cell == cell)
            src = total.at[g, colour, t]
            dst = tiles.at[kind, index, where % 2]
            act(src, dst, kind, here, (to_grp, to_cell))

    def start_tile(src, dst, kind, here, target):
        @pl.when(here)
        def _():
            pltpu.make_async_copy(src, dst, tile_recv.at[kind]).start()

        @pl.when(jnp.logical_not(here))
        def _():
            copy_to(src, dst, tile_send, tile_recv.at[kind], target).start()

    def finish_tile(src, dst, kind, here, target):
        @pl.when(jnp.logical_not(here))
        def _():
            copy_to(src, dst, tile_send, tile_recv.at[kind], target).wait_send()

    for g in range(3):
        for colour in range(2):
            here = z if colour == 0 else y
            seven = arrived.at[g, colour, pl.ds(0, 7)]
            copy_to(seven, seven, ring_send.at[g, colour], ring_recv.at[g, colour], peer).wait_recv()
            acc = part[g, core, colour, here]
            for d in range(1, 8):
                acc = acc + arrived[g, colour, (here + d) % 8]
            total[g, colour] = acc
            for t in range(2):
                tile_copies(g, colour, t, start_tile)

    apart = (cell // 8 - x) % 4
    for kind in range(2):
        used = apart != 3 if kind == 0 else apart >= 2

        @pl.when(used)
        def _(kind=kind):
            whole = tiles.at[kind]
            copy_to(whole, whole, tile_send, tile_recv.at[kind], peer).wait_recv()
            mine[kind] = jnp.sum(tiles[kind], axis=0)

        @pl.when(jnp.logical_not(used))
        def _(kind=kind):
            mine[kind] = jnp.zeros_like(mine[kind])

    last = copy_to(mine, other, last_send, last_recv, peer)
    last.start()

    for q in (1, 2, 3):
        y_copy(other_y(q)).wait_send()
    for q in range(4):
        x1_copy(q).wait_send()
        x2_copy(q).wait_send()
    for g in range(3):
        core_copy(g).wait_send()
        for colour in range(2):
            seven = arrived.at[g, colour, pl.ds(0, 7)]
            copy_to(seven, seven, ring_send.at[g, colour], ring_recv.at[g, colour], peer).wait_send()
            for t in range(2):
                tile_copies(g, colour, t, finish_tile)

    last.wait()
    first = core == 0
    low = jnp.where(first, mine[...], other[...])
    high = jnp.where(first, other[...], mine[...])

    def whole_tile(kind):
        return jnp.concatenate([low[kind, 0], high[kind, 0], low[kind, 1], high[kind, 1]], axis=0)

    full = (whole_tile(0) + whole_tile(1).T) * (1.0 / CELLS)
    out_ref[...] = jnp.where(first, full[:, :64], full[:, 64:])


def body(snapshots, density):
    f32, bf16, dma = jnp.float32, jnp.bfloat16, pltpu.SemaphoreType.DMA
    return pl.pallas_call(
        kernel,
        out_shape=jax.ShapeDtypeStruct((128, 64), f32),
        in_specs=[pl.BlockSpec(memory_space=pl.ANY), pl.BlockSpec(memory_space=pltpu.SMEM)],
        out_specs=pl.BlockSpec(memory_space=pltpu.VMEM),
        scratch_shapes=[
            pltpu.VMEM((SLAB, SNAP), bf16),
            pltpu.VMEM((4, SNAP, QUARTER), bf16),
            pltpu.VMEM((4, SNAP, QUARTER), bf16),
            pltpu.VMEM((4, SNAP, QUARTER), bf16),
            pltpu.VMEM((4, SNAP, HALF), bf16),
            pltpu.VMEM((3, 2, 2, 8, 2, 32, 128), f32),
            pltpu.VMEM((3, 2, 8, 2, 32, 128), f32),
            pltpu.VMEM((3, 2, 8, 2, 32, 128), f32),
            pltpu.VMEM((3, 2, 2, 32, 128), f32),
            pltpu.VMEM((2, 8, 2, 32, 128), f32),
            pltpu.VMEM((2, 2, 32, 128), f32),
            pltpu.VMEM((2, 2, 32, 128), f32),
            dma, dma((4,)), dma((4,)), dma((4,)), dma((4,)), dma((4,)), dma((4,)), dma((3,)), dma((3,)),
            dma((3, 2)), dma((3, 2)), dma, dma((2,)), dma, dma,
            pltpu.SemaphoreType.REGULAR, pltpu.SemaphoreType.REGULAR,
        ],
        compiler_params=pltpu.CompilerParams(
            collective_id=0, has_side_effects=True, vmem_limit_bytes=40 * 2**20
        ),
        cost_estimate=pl.CostEstimate(flops=10**9, bytes_accessed=10**6, transcendentals=0),
    )(snapshots, density)


def solution(mesh):
    in_specs = (P("cell", "grp"), P())
    return jax.shard_map(body, mesh=mesh, in_specs=in_specs, out_specs=P("grp", "cell"), check_vma=False)
```

time: 434 us -> 103 us (0.24)
  the two profiles are of different devices: /device:TPU:4 before, /device:TPU:85 now
where the time goes in v1:
time: 103 us
  Pallas kernels  101 us (98%)
  local copies, waits for them, and re-layouts  2.49 us (2%)
    pallas_call x1, Pallas kernels, body(): pl.pallas_call(kernel, out_shape=jax.ShapeDtypeStruct((128, 64), f32), in...  101 us

profile of v1, /device:TPU:85, one launch (start us, length us, event | category | flops | bytes accessed | tf_op | source)
XLA Modules:
  0.0 103.3 jit_solution(14316026778896765442)
XLA Ops:
  0.0 0.0 copy-start
  0.0 1.1 %copy-done = bf16[3072,128]{1,0:T(8,128)(2,1)S(1)} copy-done((bf16[3072,128]{1,0:T(8,128)(2,1)S(1)}, bf16[3072,128]{1,0:T(8,128)(2,1)}, u32[]{:S(2)}) %copy-start) | copy-done | bytes 786456
  1.1 0.0 copy-start.1
  1.1 0.7 copy-done.1
  1.8 100.8 %shard_map.28 = f32[128,64]{1,0:T(8,128)S(1)} custom-call(bf16[3072,128]{1,0:T(8,128)(2,1)S(1)} %copy-done, f32[8]{0:T(128)S(1)} %copy-done.1), custom_call_target="tpu_custom_call" | custom-call | flops 1000000000 | bytes 1000000 | tf_op jit(solution)/shard_map/pallas_call | solution.py:251
  102.6 0.7 copy.3
Async XLA Ops:
  0.0 1.1 %copy-start = (bf16[3072,128]{1,0:T(8,128)(2,1)S(1)}, bf16[3072,128]{1,0:T(8,128)(2,1)}, u32[]{:S(2)}) copy-start(bf16[3072,128]{1,0:T(8,128)(2,1)} %snap_hbm.1) | copy-start | bytes 2359300
  1.1 0.7 copy-start.1

commit v2 on v1

--- a/solution.py
+++ b/solution.py
@@ -25,9 +25,9 @@
 
 def kernel(
     snap_hbm, density_ref, out_ref,
-    snap, turned, own, next1, next2, part, peer_part, arrived, total, tiles, mine, other,
+    snap, turned, own, next1, next2, part, peer_part, arrived, total, crossed, piece, mine, other,
     load_sem, y_send, y_recv, x1_send, x1_recv, x2_send, x2_recv, core_send, core_recv,
-    ring_send, ring_recv, tile_send, tile_recv, last_send, last_recv, plane_sem, all_sem,
+    ring_send, ring_recv, cross_send, cross_recv, tile_send, tile_recv, last_send, last_recv, plane_sem, all_sem,
 ):
     grp, cell = lax.axis_index("grp"), lax.axis_index("cell")
     x, ylo, z, core = grp // 4, grp % 4, cell // 4, cell % 2
@@ -164,18 +164,42 @@
     spread(2)
     pl.semaphore_wait(all_sem, 3)
 
-    def tile_copies(g, colour, t, act):
-        k = 2 * colour + t
+    def cross_copy(colour, d):
+        if colour == 0:
+            here, there = y, (y + d) % 8
+            target = device(x, there, z, core)
+        else:
+            here, there = z, (z + d) % 8
+            target = device(x, y, there, core)
+        return copy_to(
+            total.at[colour, there], crossed.at[colour, here], cross_send.at[colour], cross_recv.at[colour], target
+        )
+
+    for colour in range(2):
+        here = z if colour == 0 else y
+        for g in range(3):
+            seven = arrived.at[g, colour, pl.ds(0, 7)]
+            copy_to(seven, seven, ring_send.at[g, colour], ring_recv.at[g, colour], peer).wait_recv()
+            acc = part[g, core, colour, here]
+            for d in range(1, 8):
+                acc = acc + arrived[g, colour, (here + d) % 8]
+            total[colour, :, g] = acc.reshape(8, 8, 128)
+
+        @pl.loop(1, 8)
+        def _(d):
+            cross_copy(colour, d).start()
+
+    def tile_copies(colour, g, act):
         where, index = (z, y) if colour == 0 else (y, z)
         row = x * 4 + where // 2
-        column = ((x + g) % 4) * 4 + k
+        column = ((x + g) % 4) * 4 + 2 * colour + index // 4
         targets = [(0, row, 2 * column + core)]
         if g > 0:
             targets.append((1, column, 2 * row + core))
         for kind, to_grp, to_cell in targets:
             here = jnp.logical_and(to_grp == grp, to_cell == cell)
-            src = total.at[g, colour, t]
-            dst = tiles.at[kind, index, where % 2]
+            src = piece.at[colour, g]
+            dst = mine.at[kind, where % 2, index % 4]
             act(src, dst, kind, here, (to_grp, to_cell))
 
     def start_tile(src, dst, kind, here, target):
@@ -192,17 +216,16 @@
         def _():
             copy_to(src, dst, tile_send, tile_recv.at[kind], target).wait_send()
 
-    for g in range(3):
-        for colour in range(2):
-            here = z if colour == 0 else y
-            seven = arrived.at[g, colour, pl.ds(0, 7)]
-            copy_to(seven, seven, ring_send.at[g, colour], ring_recv.at[g, colour], peer).wait_recv()
-            acc = part[g, core, colour, here]
-            for d in range(1, 8):
-                acc = acc + arrived[g, colour, (here + d) % 8]
-            total[g, colour] = acc
-            for t in range(2):
-                tile_copies(g, colour, t, start_tile)
+    for colour in range(2):
+        here = y if colour == 0 else z
+        seven = crossed.at[colour, pl.ds(0, 7)]
+        copy_to(seven, seven, cross_send.at[colour], cross_recv.at[colour], peer).wait_recv()
+        acc = total[colour, here]
+        for d in range(1, 8):
+            acc = acc + crossed[colour, (here + d) % 8]
+        piece[colour] = acc
+        for g in range(3):
+            tile_copies(colour, g, start_tile)
 
     apart = (cell // 8 - x) % 4
     for kind in range(2):
@@ -210,9 +233,8 @@
 
         @pl.when(used)
         def _(kind=kind):
-            whole = tiles.at[kind]
+            whole = mine.at[kind]
             copy_to(whole, whole, tile_send, tile_recv.at[kind], peer).wait_recv()
-            mine[kind] = jnp.sum(tiles[kind], axis=0)
 
         @pl.when(jnp.logical_not(used))
         def _(kind=kind):
@@ -231,13 +253,15 @@
         for colour in range(2):
             seven = arrived.at[g, colour, pl.ds(0, 7)]
             copy_to(seven, seven, ring_send.at[g, colour], ring_recv.at[g, colour], peer).wait_send()
-            for t in range(2):
-                tile_copies(g, colour, t, finish_tile)
+            tile_copies(colour, g, finish_tile)
+    for colour in range(2):
+        seven = crossed.at[colour, pl.ds(0, 7)]
+        copy_to(seven, seven, cross_send.at[colour], cross_recv.at[colour], peer).wait_send()
 
     last.wait()
     first = core == 0
-    low = jnp.where(first, mine[...], other[...])
-    high = jnp.where(first, other[...], mine[...])
+    low = jnp.where(first, mine[...], other[...]).reshape(2, 2, 32, 128)
+    high = jnp.where(first, other[...], mine[...]).reshape(2, 2, 32, 128)
 
     def whole_tile(kind):
         return jnp.concatenate([low[kind, 0], high[kind, 0], low[kind, 1], high[kind, 1]], axis=0)
@@ -262,12 +286,13 @@
             pltpu.VMEM((3, 2, 2, 8, 2, 32, 128), f32),
             pltpu.VMEM((3, 2, 8, 2, 32, 128), f32),
             pltpu.VMEM((3, 2, 8, 2, 32, 128), f32),
-            pltpu.VMEM((3, 2, 2, 32, 128), f32),
-            pltpu.VMEM((2, 8, 2, 32, 128), f32),
-            pltpu.VMEM((2, 2, 32, 128), f32),
-            pltpu.VMEM((2, 2, 32, 128), f32),
+            pltpu.VMEM((2, 8, 3, 8, 128), f32),
+            pltpu.VMEM((2, 8, 3, 8, 128), f32),
+            pltpu.VMEM((2, 3, 8, 128), f32),
+            pltpu.VMEM((2, 2, 4, 8, 128), f32),
+            pltpu.VMEM((2, 2, 4, 8, 128), f32),
             dma, dma((4,)), dma((4,)), dma((4,)), dma((4,)), dma((4,)), dma((4,)), dma((3,)), dma((3,)),
-            dma((3, 2)), dma((3, 2)), dma, dma((2,)), dma, dma,
+            dma((3, 2)), dma((3, 2)), dma((2,)), dma((2,)), dma, dma((2,)), dma, dma,
             pltpu.SemaphoreType.REGULAR, pltpu.SemaphoreType.REGULAR,
         ],
         compiler_params=pltpu.CompilerParams(

time: 103 us -> 85.8 us (0.83)
  the two profiles are of different devices: /device:TPU:85 before, /device:TPU:29 now
where the time goes in v2:
time: 85.8 us; the launch traced here: 85.6 us
  Pallas kernels  83.2 us (97%)
  local copies, waits for them, and re-layouts  2.49 us (3%)
    pallas_call x1, Pallas kernels, body(): pl.pallas_call(kernel, out_shape=jax.ShapeDtypeStruct((128, 64), f32), in...  83.2 us
    unnamed x4, local copies, waits for them, and re-layouts  1.79 us

profile of v2, /device:TPU:29, one launch (start us, length us, event | category | flops | bytes accessed | tf_op | source)
XLA Modules:
  0.0 85.6 jit_solution(15197605821484202624)
XLA Ops:
  0.0 0.0 copy-start
  0.0 1.1 %copy-done = bf16[3072,128]{1,0:T(8,128)(2,1)S(1)} copy-done((bf16[3072,128]{1,0:T(8,128)(2,1)S(1)}, bf16[3072,128]{1,0:T(8,128)(2,1)}, u32[]{:S(2)}) %copy-start) | copy-done | bytes 786456
  1.1 0.0 copy-start.1
  1.1 0.7 copy-done.1
  1.8 83.2 %shard_map.28 = f32[128,64]{1,0:T(8,128)S(1)} custom-call(bf16[3072,128]{1,0:T(8,128)(2,1)S(1)} %copy-done, f32[8]{0:T(128)S(1)} %copy-done.1), custom_call_target="tpu_custom_call" | custom-call | flops 1000000000 | bytes 1000000 | tf_op jit(solution)/shard_map/pallas_call | solution.py:275
  84.9 0.7 copy.3
Async XLA Ops:
  0.0 1.1 %copy-start = (bf16[3072,128]{1,0:T(8,128)(2,1)S(1)}, bf16[3072,128]{1,0:T(8,128)(2,1)}, u32[]{:S(2)}) copy-start(bf16[3072,128]{1,0:T(8,128)(2,1)} %snap_hbm.1) | copy-start | bytes 2359300
  1.1 0.7 copy-start.1

commit v3 on v2

--- a/solution.py
+++ b/solution.py
@@ -9,7 +9,10 @@
 CELLS = 98304
 SLAB = 3072
 QUARTER = SLAB // 4
-HALF = QUARTER // 2
+CHUNKS = 3
+AHEAD = 1
+WIDE = QUARTER // CHUNKS
+NARROW = WIDE // 2
 SNAP = 128
 
 
@@ -25,8 +28,8 @@
 
 def kernel(
     snap_hbm, density_ref, out_ref,
-    snap, turned, own, next1, next2, part, peer_part, arrived, total, crossed, piece, mine, other,
-    load_sem, y_send, y_recv, x1_send, x1_recv, x2_send, x2_recv, core_send, core_recv,
+    snap, turned, own, next1, passing, next2, part, peer_part, arrived, total, crossed, piece, mine, other,
+    load_sem, y_send, y_recv, x1_send, x1_recv, pass_send, pass_recv, x2_send, x2_recv, core_send, core_recv,
     ring_send, ring_recv, cross_send, cross_recv, tile_send, tile_recv, last_send, last_recv, plane_sem, all_sem,
 ):
     grp, cell = lax.axis_index("grp"), lax.axis_index("cell")
@@ -58,59 +61,75 @@
     load.wait()
     scale = jnp.sqrt(jnp.full((1, SNAP), density_ref[z], jnp.float32))
     for q in range(4):
-        block = snap[pl.ds(q * QUARTER, QUARTER), :].astype(jnp.float32) * scale
-        turned[q] = block.astype(jnp.bfloat16).T
-    own[ylo] = turned[ylo]
+        for c in range(CHUNKS):
+            block = snap[pl.ds(q * QUARTER + c * WIDE, WIDE), :].astype(jnp.float32) * scale
+            turned[q, c] = block.astype(jnp.bfloat16).T
+    for c in range(CHUNKS):
+        own[c, ylo] = turned[ylo, c]
     pl.semaphore_wait(barrier, 18)
-
-    def y_copy(q):
-        return copy_to(
-            turned.at[q], own.at[ylo], y_send.at[q], y_recv.at[ylo], device(x, y_base + q, z, core)
-        )
-
-    def y_arrival(q):
-        return copy_to(turned.at[q], own.at[q], y_send.at[q], y_recv.at[q], device(x, y_base + q, z, core))
 
     def other_y(d):
         return (ylo + d) % 4
 
-    for d in (1, 2, 3):
-        y_copy(other_y(d)).start()
+    def y_copy(c, q):
+        return copy_to(
+            turned.at[q, c], own.at[c, ylo], y_send.at[c, q], y_recv.at[c, ylo], device(x, y_base + q, z, core)
+        )
+
+    def y_arrival(c, q):
+        return copy_to(
+            turned.at[q, c], own.at[c, q], y_send.at[c, q], y_recv.at[c, q], device(x, y_base + q, z, core)
+        )
 
     half = x // 2
     half_next2 = ((x + 2) % 4) // 2
 
-    def x1_copy(q):
-        return copy_to(
-            own.at[q], next1.at[q], x1_send.at[q], x1_recv.at[q], device((x + 3) % 4, y, z, core)
-        )
-
-    def x2_copy(q):
-        lanes = pl.ds(pl.multiple_of(half_next2 * HALF, HALF), HALF)
-        return copy_to(
-            own.at[q, :, lanes], next2.at[q], x2_send.at[q], x2_recv.at[q], device((x + 2) % 4, y, z, core)
-        )
-
-    x1_copy(ylo).start()
-    x2_copy(ylo).start()
+    def x1_copy(c):
+        return copy_to(own.at[c], next1.at[c], x1_send.at[c], x1_recv.at[c], device((x + 3) % 4, y, z, core))
+
+    def pass_copy(c):
+        lanes = pl.ds(pl.multiple_of(half_next2 * NARROW, NARROW), NARROW)
+        return copy_to(
+            own.at[c, :, :, lanes], passing.at[c], pass_send.at[c], pass_recv.at[c], device((x + 1) % 4, y, z, core)
+        )
+
+    def x2_copy(c):
+        return copy_to(
+            passing.at[c], next2.at[c], x2_send.at[c], x2_recv.at[c], device((x + 1) % 4, y, z, core)
+        )
+
+    for c in range(AHEAD):
+        for d in (1, 2, 3):
+            y_copy(c, other_y(d)).start()
 
     for d in range(1, 8):
         greet(plane_sem, d, "y")
 
-    for d in (1, 2, 3):
-        q = other_y(d)
-        y_arrival(q).wait_recv()
-        x1_copy(q).start()
-        x2_copy(q).start()
+    for c in range(CHUNKS):
+        for d in (1, 2, 3):
+            y_arrival(c, other_y(d)).wait_recv()
+        if c + AHEAD < CHUNKS:
+            for d in (1, 2, 3):
+                y_copy(c, other_y(d)).wait_send()
+            for d in (1, 2, 3):
+                y_copy(c + AHEAD, other_y(d)).start()
+        x1_copy(c).start()
+        pass_copy(c).start()
+        if c > 0:
+            pass_copy(c - 1).wait_recv()
+            x2_copy(c - 1).start()
 
     pl.semaphore_wait(plane_sem, 7)
     for d in range(1, 4):
         greet(all_sem, d, "x")
 
     def multiply(g, left, right):
-        product = lax.dot_general(
-            left, right, (((1,), (1,)), ((), ())), preferred_element_type=jnp.float32
-        )
+        product = None
+        for c in range(CHUNKS):
+            term = lax.dot_general(
+                left(c), right(c), (((1,), (1,)), ((), ())), preferred_element_type=jnp.float32
+            )
+            product = term if product is None else product + term
         for n in range(8):
             for h in range(2):
                 for t in range(4):
@@ -145,20 +164,25 @@
             ring_copy(g, 0, d).start()
             ring_copy(g, 1, d).start()
 
-    left = own[...].reshape(512, QUARTER)
-    multiply(0, left, left)
+    def mine_at(c):
+        return own[c].reshape(512, WIDE)
+
+    multiply(0, mine_at, mine_at)
     core_copy(0).start()
 
-    for q in range(4):
-        x1_copy(q).wait_recv()
-    multiply(1, own[...].reshape(512, QUARTER), next1[...].reshape(512, QUARTER))
+    pass_copy(CHUNKS - 1).wait_recv()
+    x2_copy(CHUNKS - 1).start()
+    spread(0)
+
+    for c in range(CHUNKS):
+        x1_copy(c).wait_recv()
+    multiply(1, mine_at, lambda c: next1[c].reshape(512, WIDE))
     core_copy(1).start()
-    spread(0)
-
-    for q in range(4):
-        x2_copy(q).wait_recv()
-    lanes = pl.ds(pl.multiple_of(half * HALF, HALF), HALF)
-    multiply(2, own[:, :, lanes].reshape(512, HALF), next2[...].reshape(512, HALF))
+
+    for c in range(CHUNKS):
+        x2_copy(c).wait_recv()
+    lanes = pl.ds(pl.multiple_of(half * NARROW, NARROW), NARROW)
+    multiply(2, lambda c: own[c, :, :, lanes].reshape(512, NARROW), lambda c: next2[c].reshape(512, NARROW))
     core_copy(2).start()
     spread(1)
     spread(2)
@@ -243,11 +267,13 @@
     last = copy_to(mine, other, last_send, last_recv, peer)
     last.start()
 
-    for q in (1, 2, 3):
-        y_copy(other_y(q)).wait_send()
-    for q in range(4):
-        x1_copy(q).wait_send()
-        x2_copy(q).wait_send()
+    for c in range(CHUNKS):
+        if c + AHEAD >= CHUNKS:
+            for d in (1, 2, 3):
+                y_copy(c, other_y(d)).wait_send()
+        x1_copy(c).wait_send()
+        pass_copy(c).wait_send()
+        x2_copy(c).wait_send()
     for g in range(3):
         core_copy(g).wait_send()
         for colour in range(2):
@@ -279,10 +305,11 @@
         out_specs=pl.BlockSpec(memory_space=pltpu.VMEM),
         scratch_shapes=[
             pltpu.VMEM((SLAB, SNAP), bf16),
-            pltpu.VMEM((4, SNAP, QUARTER), bf16),
-            pltpu.VMEM((4, SNAP, QUARTER), bf16),
-            pltpu.VMEM((4, SNAP, QUARTER), bf16),
-            pltpu.VMEM((4, SNAP, HALF), bf16),
+            pltpu.VMEM((4, CHUNKS, SNAP, WIDE), bf16),
+            pltpu.VMEM((CHUNKS, 4, SNAP, WIDE), bf16),
+            pltpu.VMEM((CHUNKS, 4, SNAP, WIDE), bf16),
+            pltpu.VMEM((CHUNKS, 4, SNAP, NARROW), bf16),
+            pltpu.VMEM((CHUNKS, 4, SNAP, NARROW), bf16),
             pltpu.VMEM((3, 2, 2, 8, 2, 32, 128), f32),
             pltpu.VMEM((3, 2, 8, 2, 32, 128), f32),
             pltpu.VMEM((3, 2, 8, 2, 32, 128), f32),
@@ -291,12 +318,12 @@
             pltpu.VMEM((2, 3, 8, 128), f32),
             pltpu.VMEM((2, 2, 4, 8, 128), f32),
             pltpu.VMEM((2, 2, 4, 8, 128), f32),
-            dma, dma((4,)), dma((4,)), dma((4,)), dma((4,)), dma((4,)), dma((4,)), dma((3,)), dma((3,)),
+            dma, dma((CHUNKS, 4)), dma((CHUNKS, 4)), *[dma((CHUNKS,))] * 6, dma((3,)), dma((3,)),
             dma((3, 2)), dma((3, 2)), dma((2,)), dma((2,)), dma, dma((2,)), dma, dma,
             pltpu.SemaphoreType.REGULAR, pltpu.SemaphoreType.REGULAR,
         ],
         compiler_params=pltpu.CompilerParams(
-            collective_id=0, has_side_effects=True, vmem_limit_bytes=40 * 2**20
+            collective_id=0, has_side_effects=True, vmem_limit_bytes=60 * 2**20
         ),
         cost_estimate=pl.CostEstimate(flops=10**9, bytes_accessed=10**6, transcendentals=0),
     )(snapshots, density)

time: 85.8 us -> 76 us (0.89)
  the two profiles are of different devices: /device:TPU:29 before, /device:TPU:61 now
where the time goes in v3:
time: 76 us; the launch traced here: 75.8 us
  Pallas kernels  74.2 us (98%)
  local copies, waits for them, and re-layouts  1.54 us (2%)
    pallas_call x1, Pallas kernels, body(): pl.pallas_call(kernel, out_shape=jax.ShapeDtypeStruct((128, 64), f32), in...  74.2 us
    pallas_call x1, local copies, waits for them, and re-layouts, body(): pl.pallas_call(kernel, out_shape=jax.ShapeDtypeStruct((128, 64), f32), in...  1.54 us

profile of v3, /device:TPU:61, one launch (start us, length us, event | category | flops | bytes accessed | tf_op | source)
XLA Modules:
  0.0 75.8 jit_solution(9334909301187067660)
XLA Ops:
  0.0 74.2 %shard_map.28 = f32[128,64]{1,0:T(8,128)} custom-call(bf16[3072,128]{1,0:T(8,128)(2,1)} %snap_hbm.1, f32[8]{0:T(128)} %density_ref.1), custom_call_target="tpu_custom_call" | custom-call | flops 1000000000 | bytes 1000000 | tf_op jit(solution)/shard_map/pallas_call | solution.py:301
  74.2 1.5 %copy.3 = f32[128,64]{0,1:T(8,128)} copy(f32[128,64]{1,0:T(8,128)} %shard_map.28) | data formatting | bytes 65536 | tf_op jit(solution)/shard_map/pallas_call | solution.py:301

commit v4 on v3

v4 whole, which is shorter than its diff:
```python
import jax
import jax.numpy as jnp
from jax import lax
from jax.experimental import pallas as pl
from jax.experimental.pallas import tpu as pltpu
from jax.sharding import PartitionSpec as P

MESH = pl.DeviceIdType.MESH
CELLS = 98304
SLAB = 3072
QUARTER = SLAB // 4
CHUNKS = 6
HALF = CHUNKS // 2
AHEAD = 2
WIDE = QUARTER // CHUNKS
SNAP = 128


def device(x, y, z, core):
    return x * 4 + y % 4, (z * 2 + y // 4) * 2 + core


def copy_to(src, dst, send, recv, target):
    return pltpu.make_async_remote_copy(
        src_ref=src, dst_ref=dst, send_sem=send, recv_sem=recv, device_id=target, device_id_type=MESH
    )


def kernel(
    snap_hbm, density_ref, out_ref,
    snap, turned, own, next1, passing, next2, part, peer_part, between, arrived, total, crossed, piece, mine, other,
    load_sem, y_send, y_recv, x1_send, x1_recv, pass_send, pass_recv, x2_send, x2_recv, core_send, core_recv,
    line_send, between_recv, arrived_recv, cross_send, cross_recv, tile_send, tile_recv, last_send, last_recv, plane_sem, all_sem,
):
    grp, cell = lax.axis_index("grp"), lax.axis_index("cell")
    x, ylo, z, core = grp // 4, grp % 4, cell // 4, cell % 2
    y = (cell // 2) % 2 * 4 + ylo
    y_base = y - ylo
    peer = (grp, cell + 1 - 2 * core)

    load = pltpu.make_async_copy(snap_hbm, snap, load_sem)
    load.start()

    barrier = pltpu.get_barrier_semaphore()

    def greet(sem, d, axis):
        target = {
            "x": lambda: device((x + d) % 4, y, z, core),
            "y": lambda: device(x, (y + d) % 8, z, core),
            "z": lambda: device(x, y, (z + d) % 8, core),
        }[axis]()
        pl.semaphore_signal(sem, inc=1, device_id=target, device_id_type=MESH)

    for d in range(1, 4):
        greet(barrier, d, "x")
    for d in range(1, 8):
        greet(barrier, d, "y")
        greet(barrier, d, "z")
    pl.semaphore_signal(barrier, inc=1, device_id=peer, device_id_type=MESH)

    half = x // 2
    first_chunk = (1 - half) * HALF

    def chunk(n):
        return (n + first_chunk) % CHUNKS

    load.wait()
    scale = jnp.sqrt(jnp.full((1, SNAP), density_ref[z], jnp.float32))

    def weigh(c):
        for q in range(4):
            rows = pl.ds(pl.multiple_of(q * QUARTER + c * WIDE, WIDE), WIDE)
            turned[q, c] = (snap[rows, :].astype(jnp.float32) * scale).astype(jnp.bfloat16).T
        own[c, ylo] = turned[ylo, c]

    def other_y(d):
        return (ylo + d) % 4

    def y_copy(c, q):
        return copy_to(
            turned.at[q, c], own.at[c, ylo], y_send.at[c, q], y_recv.at[c, ylo], device(x, y_base + q, z, core)
        )

    def y_arrival(c, q):
        return copy_to(
            turned.at[q, c], own.at[c, q], y_send.at[c, q], y_recv.at[c, q], device(x, y_base + q, z, core)
        )

    def x1_copy(c):
        return copy_to(own.at[c], next1.at[c], x1_send.at[c], x1_recv.at[c], device((x + 3) % 4, y, z, core))

    def pass_copy(n):
        return copy_to(
            own.at[chunk(n)], passing.at[n], pass_send.at[n], pass_recv.at[n], device((x + 1) % 4, y, z, core)
        )

    def x2_copy(n):
        return copy_to(
            passing.at[n], next2.at[n], x2_send.at[n], x2_recv.at[n], device((x + 1) % 4, y, z, core)
        )

    def start_y(n):
        for d in (1, 2, 3):
            y_copy(chunk(n), other_y(d)).start()

    for n in range(AHEAD):
        weigh(chunk(n))
    pl.semaphore_wait(barrier, 18)
    for n in range(AHEAD):
        start_y(n)
    for n in range(AHEAD, CHUNKS):
        weigh(chunk(n))

    for d in range(1, 8):
        greet(plane_sem, d, "y")

    for n in range(CHUNKS):
        for d in (1, 2, 3):
            y_arrival(chunk(n), other_y(d)).wait_recv()
        if n + AHEAD < CHUNKS:
            for d in (1, 2, 3):
                y_copy(chunk(n), other_y(d)).wait_send()
            start_y(n + AHEAD)
        x1_copy(chunk(n)).start()
        if n < HALF:
            pass_copy(n).start()
        if 2 <= n < HALF + 2:
            pass_copy(n - 2).wait_recv()
            x2_copy(n - 2).start()

    pl.semaphore_wait(plane_sem, 7)
    for d in range(1, 4):
        greet(all_sem, d, "x")

    def multiply(g, chunks, left, right):
        product = None
        for c in range(chunks):
            term = lax.dot_general(
                left(c).reshape(512, WIDE), right(c).reshape(512, WIDE), (((1,), (1,)), ((), ())),
                preferred_element_type=jnp.float32,
            )
            product = term if product is None else product + term
        for n in range(8):
            for h in range(2):
                for t in range(4):
                    part[g, h, t // 2, n, t % 2] = product[
                        n * 64 + h * 32 : n * 64 + h * 32 + 32, t * 128 : t * 128 + 128
                    ]

    def core_copy(g):
        return copy_to(part.at[g, 1 - core], peer_part.at[g], core_send.at[g], core_recv.at[g], peer)

    def place(colour):
        return z if colour == 0 else y

    def at_line(colour, d):
        there = (place(colour) + d + 8) % 8
        return there, device(x, y, there, core) if colour == 0 else device(x, there, z, core)

    def line_copy(g, colour, src, dst, recv, target):
        return copy_to(src, dst, line_send.at[g, colour], recv.at[g, colour], target)

    def spread(g):
        core_copy(g).wait_recv()
        part[g, core] = part[g, core] + peer_part[g]
        for colour in range(2):
            terms = part.at[g, core, colour]
            for s, way in ((0, 1), (1, -1)):
                beside, target = at_line(colour, way)
                third, _ = at_line(colour, 3 * way)
                fourth, _ = at_line(colour, 4)
                _, target2 = at_line(colour, 2 * way)
                slot = between.at[g, colour, s]
                line_copy(g, colour, terms.at[third], slot.at[pl.ds(0, 2)], between_recv, target).start()
                line_copy(g, colour, terms.at[fourth, s], slot.at[2], between_recv, target2).start()
        for colour in range(2):
            terms = part.at[g, core, colour]
            for s, way in ((0, 1), (1, -1)):
                beside, target = at_line(colour, way)
                line_copy(g, colour, terms.at[beside], arrived.at[g, colour, s], arrived_recv, target).start()

    def send_on(g):
        for colour in range(2):
            terms = part.at[g, core, colour]
            whole = between.at[g, colour]
            line_copy(g, colour, whole, whole, between_recv, peer).wait_recv()
            for s, way in ((0, 1), (1, -1)):
                there, target = at_line(colour, 2 * way)
                terms[there] = terms[there] + between[g, colour, s, :2]
                terms[there, s] = terms[there, s] + between[g, colour, s, 2]
                line_copy(g, colour, terms.at[there], arrived.at[g, colour, 2 + s], arrived_recv, target).start()

    multiply(0, CHUNKS, lambda c: own[c], lambda c: own[c])
    core_copy(0).start()

    for n in range(HALF):
        x2_copy(n).wait_recv()
    multiply(2, HALF, lambda n: own[half * HALF + n], lambda n: next2[n])
    core_copy(2).start()
    spread(0)
    spread(2)

    for c in range(CHUNKS):
        x1_copy(c).wait_recv()
    multiply(1, CHUNKS, lambda c: own[c], lambda c: next1[c])
    core_copy(1).start()
    spread(1)
    send_on(0)
    send_on(2)
    send_on(1)
    pl.semaphore_wait(all_sem, 3)

    def cross_copy(colour, d):
        if colour == 0:
            here, there = y, (y + d) % 8
            target = device(x, there, z, core)
        else:
            here, there = z, (z + d) % 8
            target = device(x, y, there, core)
        return copy_to(
            total.at[colour, there], crossed.at[colour, here], cross_send.at[colour], cross_recv.at[colour], target
        )

    for n in range(CHUNKS):
        if n + AHEAD >= CHUNKS:
            for d in (1, 2, 3):
                y_copy(chunk(n), other_y(d)).wait_send()
        x1_copy(n).wait_send()
        if n < HALF:
            pass_copy(n).wait_send()
            x2_copy(n).wait_send()
    for g in range(3):
        core_copy(g).wait_send()

    for colour in range(2):
        here = z if colour == 0 else y
        for g in range(3):
            whole = arrived.at[g, colour]
            line_copy(g, colour, whole, whole, arrived_recv, peer).wait_recv()
            acc = part[g, core, colour, here]
            for d in range(4):
                acc = acc + arrived[g, colour, d]
            total[colour, :, g] = acc.reshape(8, 8, 128)

        @pl.loop(1, 8)
        def _(d):
            cross_copy(colour, d).start()

    def tile_copies(colour, g, act):
        where, index = (z, y) if colour == 0 else (y, z)
        row = x * 4 + where // 2
        column = ((x + g) % 4) * 4 + 2 * colour + index // 4
        targets = [(0, row, 2 * column + core)]
        if g > 0:
            targets.append((1, column, 2 * row + core))
        for kind, to_grp, to_cell in targets:
            here = jnp.logical_and(to_grp == grp, to_cell == cell)
            src = piece.at[colour, g]
            dst = mine.at[kind, where % 2, index % 4]
            act(src, dst, kind, here, (to_grp, to_cell))

    def start_tile(src, dst, kind, here, target):
        @pl.when(here)
        def _():
            pltpu.make_async_copy(src, dst, tile_recv.at[kind]).start()

        @pl.when(jnp.logical_not(here))
        def _():
            copy_to(src, dst, tile_send, tile_recv.at[kind], target).start()

    def finish_tile(src, dst, kind, here, target):
        @pl.when(jnp.logical_not(here))
        def _():
            copy_to(src, dst, tile_send, tile_recv.at[kind], target).wait_send()

    for colour in range(2):
        here = y if colour == 0 else z
        seven = crossed.at[colour, pl.ds(0, 7)]
        copy_to(seven, seven, cross_send.at[colour], cross_recv.at[colour], peer).wait_recv()
        acc = total[colour, here]
        for d in range(1, 8):
            acc = acc + crossed[colour, (here + d) % 8]
        piece[colour] = acc
        for g in range(3):
            tile_copies(colour, g, start_tile)

    apart = (cell // 8 - x) % 4
    for kind in range(2):
        used = apart != 3 if kind == 0 else apart >= 2

        @pl.when(used)
        def _(kind=kind):
            whole = mine.at[kind]
            copy_to(whole, whole, tile_send, tile_recv.at[kind], peer).wait_recv()

        @pl.when(jnp.logical_not(used))
        def _(kind=kind):
            mine[kind] = jnp.zeros_like(mine[kind])

    last = copy_to(mine, other, last_send, last_recv, peer)
    last.start()

    for g in range(3):
        for colour in range(2):
            seven = part.at[g, core, colour, pl.ds(0, 7)]
            line_copy(g, colour, seven, seven, arrived_recv, peer).wait_send()
            tile_copies(colour, g, finish_tile)
    for colour in range(2):
        seven = crossed.at[colour, pl.ds(0, 7)]
        copy_to(seven, seven, cross_send.at[colour], cross_recv.at[colour], peer).wait_send()

    last.wait()
    first = core == 0
    low = jnp.where(first, mine[...], other[...]).reshape(2, 2, 32, 128)
    high = jnp.where(first, other[...], mine[...]).reshape(2, 2, 32, 128)

    def whole_tile(kind):
        return jnp.concatenate([low[kind, 0], high[kind, 0], low[kind, 1], high[kind, 1]], axis=0)

    full = (whole_tile(0).T + whole_tile(1)) * (1.0 / CELLS)
    out_ref[...] = jnp.where(first, full[:64], full[64:])


def body(snapshots, density):
    f32, bf16, dma = jnp.float32, jnp.bfloat16, pltpu.SemaphoreType.DMA
    return pl.pallas_call(
        kernel,
        out_shape=jax.ShapeDtypeStruct((64, 128), f32),
        in_specs=[pl.BlockSpec(memory_space=pl.ANY), pl.BlockSpec(memory_space=pltpu.SMEM)],
        out_specs=pl.BlockSpec(memory_space=pltpu.VMEM),
        scratch_shapes=[
            pltpu.VMEM((SLAB, SNAP), bf16),
            pltpu.VMEM((4, CHUNKS, SNAP, WIDE), bf16),
            pltpu.VMEM((CHUNKS, 4, SNAP, WIDE), bf16),
            pltpu.VMEM((CHUNKS, 4, SNAP, WIDE), bf16),
            pltpu.VMEM((HALF, 4, SNAP, WIDE), bf16),
            pltpu.VMEM((HALF, 4, SNAP, WIDE), bf16),
            pltpu.VMEM((3, 2, 2, 8, 2, 32, 128), f32),
            pltpu.VMEM((3, 2, 8, 2, 32, 128), f32),
            pltpu.VMEM((3, 2, 2, 3, 32, 128), f32),
            pltpu.VMEM((3, 2, 4, 2, 32, 128), f32),
            pltpu.VMEM((2, 8, 3, 8, 128), f32),
            pltpu.VMEM((2, 8, 3, 8, 128), f32),
            pltpu.VMEM((2, 3, 8, 128), f32),
            pltpu.VMEM((2, 2, 4, 8, 128), f32),
            pltpu.VMEM((2, 2, 4, 8, 128), f32),
            dma, dma((CHUNKS, 4)), dma((CHUNKS, 4)), *[dma((CHUNKS,))] * 2, *[dma((HALF,))] * 4, dma((3,)), dma((3,)),
            dma((3, 2)), dma((3, 2)), dma((3, 2)), dma((2,)), dma((2,)), dma, dma((2,)), dma, dma,
            pltpu.SemaphoreType.REGULAR, pltpu.SemaphoreType.REGULAR,
        ],
        compiler_params=pltpu.CompilerParams(
            collective_id=0, has_side_effects=True, vmem_limit_bytes=60 * 2**20
        ),
        cost_estimate=pl.CostEstimate(flops=10**9, bytes_accessed=10**6, transcendentals=0),
    )(snapshots, density).T


def solution(mesh):
    in_specs = (P("cell", "grp"), P())
    return jax.shard_map(body, mesh=mesh, in_specs=in_specs, out_specs=P("grp", "cell"), check_vma=False)
```

time: 76 us -> 69.4 us (0.913)
  Pallas kernels: 74.2 us -> 67.8 us
    pallas_call x1, Pallas kernels: 74.2 us -> 67.8 us  [body(): pl.pallas_call(kernel, out_shape=jax.ShapeDtypeStruct((64, 128), f32), in...]
    pallas_call x1 -> x0, local copies, waits for them, and re-layouts: 1.54 us -> none  [body(): pl.pallas_call(kernel, out_shape=jax.ShapeDtypeStruct((128, 64), f32), in...]
    unnamed x0 -> x1, local copies, waits for them, and re-layouts: none -> 1.38 us
where the time goes in v4:
time: 69.4 us; the launch traced here: 69.1 us
  Pallas kernels  67.8 us (98%)
  local copies, waits for them, and re-layouts  1.38 us (2%)
    pallas_call x1, Pallas kernels, body(): pl.pallas_call(kernel, out_shape=jax.ShapeDtypeStruct((64, 128), f32), in...  67.8 us

profile of v4, /device:TPU:61, one launch (start us, length us, event | category | flops | bytes accessed | tf_op | source)
XLA Modules:
  0.0 69.1 jit_solution(15331658465304573696)
XLA Ops:
  0.0 67.8 %shard_map.28 = f32[64,128]{1,0:T(8,128)} custom-call(bf16[3072,128]{1,0:T(8,128)(2,1)} %snap_hbm.1, f32[8]{0:T(128)} %density_ref.1), custom_call_target="tpu_custom_call" | custom-call | flops 1000000000 | bytes 1000000 | tf_op jit(solution)/shard_map/pallas_call | solution.py:326
  67.8 1.4 %copy.4 = f32[128,64]{0,1:T(8,128)} copy(f32[128,64]{0,1:T(8,128)} %bitcast.1) | data formatting | bytes 65536

commit v5 on v4

--- a/solution.py
+++ b/solution.py
@@ -12,6 +12,8 @@
 CHUNKS = 6
 HALF = CHUNKS // 2
 AHEAD = 2
+EARLY = 4
+BATCHES = ((0, 2), (1,))
 WIDE = QUARTER // CHUNKS
 SNAP = 128
 
@@ -28,9 +30,9 @@
 
 def kernel(
     snap_hbm, density_ref, out_ref,
-    snap, turned, own, next1, passing, next2, part, peer_part, between, arrived, total, crossed, piece, mine, other,
+    snap, turned, own, next1, passing, next2, part, peer_part, between, arrived, total, crossed, piece, plain, mirror,
     load_sem, y_send, y_recv, x1_send, x1_recv, pass_send, pass_recv, x2_send, x2_recv, core_send, core_recv,
-    line_send, between_recv, arrived_recv, cross_send, cross_recv, tile_send, tile_recv, last_send, last_recv, plane_sem, all_sem,
+    line_send, between_recv, arrived_recv, cross_send, cross_recv, tile_send, tile_recv, plane_sem, all_sem,
 ):
     grp, cell = lax.axis_index("grp"), lax.axis_index("cell")
     x, ylo, z, core = grp // 4, grp % 4, cell // 4, cell % 2
@@ -103,13 +105,13 @@
         for d in (1, 2, 3):
             y_copy(chunk(n), other_y(d)).start()
 
-    for n in range(AHEAD):
-        weigh(chunk(n))
+    weigh(chunk(0))
     pl.semaphore_wait(barrier, 18)
-    for n in range(AHEAD):
-        start_y(n)
-    for n in range(AHEAD, CHUNKS):
-        weigh(chunk(n))
+    for n in range(CHUNKS):
+        if n > 0:
+            weigh(chunk(n))
+        if n < AHEAD:
+            start_y(n)
 
     for d in range(1, 8):
         greet(plane_sem, d, "y")
@@ -132,20 +134,18 @@
     for d in range(1, 4):
         greet(all_sem, d, "x")
 
-    def multiply(g, chunks, left, right):
-        product = None
-        for c in range(chunks):
-            term = lax.dot_general(
-                left(c).reshape(512, WIDE), right(c).reshape(512, WIDE), (((1,), (1,)), ((), ())),
-                preferred_element_type=jnp.float32,
-            )
-            product = term if product is None else product + term
+    def multiply(g, pairs, more=False):
+        left, right = (
+            jnp.concatenate([pair[k] for pair in pairs], axis=-1).reshape(512, len(pairs) * WIDE) for k in (0, 1)
+        )
+        product = lax.dot_general(left, right, (((1,), (1,)), ((), ())), preferred_element_type=jnp.float32)
         for n in range(8):
             for h in range(2):
                 for t in range(4):
-                    part[g, h, t // 2, n, t % 2] = product[
-                        n * 64 + h * 32 : n * 64 + h * 32 + 32, t * 128 : t * 128 + 128
-                    ]
+                    term = product[n * 64 + h * 32 : n * 64 + h * 32 + 32, t * 128 : t * 128 + 128]
+                    if more:
+                        term = term + part[g, h, t // 2, n, t % 2]
+                    part[g, h, t // 2, n, t % 2] = term
 
     def core_copy(g):
         return copy_to(part.at[g, 1 - core], peer_part.at[g], core_send.at[g], core_recv.at[g], peer)
@@ -190,19 +190,22 @@
                 terms[there, s] = terms[there, s] + between[g, colour, s, 2]
                 line_copy(g, colour, terms.at[there], arrived.at[g, colour, 2 + s], arrived_recv, target).start()
 
-    multiply(0, CHUNKS, lambda c: own[c], lambda c: own[c])
+    multiply(0, [(own[c], own[c]) for c in range(CHUNKS)])
     core_copy(0).start()
 
     for n in range(HALF):
         x2_copy(n).wait_recv()
-    multiply(2, HALF, lambda n: own[half * HALF + n], lambda n: next2[n])
+    multiply(2, [(own[half * HALF + n], next2[n]) for n in range(HALF)])
     core_copy(2).start()
     spread(0)
+
+    for n in range(EARLY):
+        x1_copy(chunk(n)).wait_recv()
+    multiply(1, [(own[chunk(n)], next1[chunk(n)]) for n in range(EARLY)])
     spread(2)
-
-    for c in range(CHUNKS):
-        x1_copy(c).wait_recv()
-    multiply(1, CHUNKS, lambda c: own[c], lambda c: next1[c])
+    for n in range(EARLY, CHUNKS):
+        x1_copy(chunk(n)).wait_recv()
+    multiply(1, [(own[chunk(n)], next1[chunk(n)]) for n in range(EARLY, CHUNKS)], more=True)
     core_copy(1).start()
     spread(1)
     send_on(0)
@@ -210,15 +213,17 @@
     send_on(1)
     pl.semaphore_wait(all_sem, 3)
 
-    def cross_copy(colour, d):
+    def cross_copy(b, colour, d):
         if colour == 0:
             here, there = y, (y + d) % 8
             target = device(x, there, z, core)
         else:
             here, there = z, (z + d) % 8
             target = device(x, y, there, core)
-        return copy_to(
-            total.at[colour, there], crossed.at[colour, here], cross_send.at[colour], cross_recv.at[colour], target
+        groups = pl.ds(2 * b, len(BATCHES[b]))
+        return copy_to(
+            total.at[colour, there, groups], crossed.at[colour, here, groups],
+            cross_send.at[b, colour], cross_recv.at[b, colour], target,
         )
 
     for n in range(CHUNKS):
@@ -232,32 +237,32 @@
     for g in range(3):
         core_copy(g).wait_send()
 
-    for colour in range(2):
-        here = z if colour == 0 else y
-        for g in range(3):
-            whole = arrived.at[g, colour]
-            line_copy(g, colour, whole, whole, arrived_recv, peer).wait_recv()
-            acc = part[g, core, colour, here]
-            for d in range(4):
-                acc = acc + arrived[g, colour, d]
-            total[colour, :, g] = acc.reshape(8, 8, 128)
-
-        @pl.loop(1, 8)
-        def _(d):
-            cross_copy(colour, d).start()
-
-    def tile_copies(colour, g, act):
+    for b, groups in enumerate(BATCHES):
+        for colour in range(2):
+            for j, g in enumerate(groups):
+                whole = arrived.at[g, colour]
+                line_copy(g, colour, whole, whole, arrived_recv, peer).wait_recv()
+                acc = part[g, core, colour, place(colour)]
+                for d in range(4):
+                    acc = acc + arrived[g, colour, d]
+                total[colour, :, 2 * b + j] = acc.reshape(8, 8, 128)
+
+            @pl.loop(1, 8)
+            def _(d):
+                cross_copy(b, colour, d).start()
+
+    def tile_copies(colour, b, j, act):
+        g = BATCHES[b][j]
         where, index = (z, y) if colour == 0 else (y, z)
         row = x * 4 + where // 2
         column = ((x + g) % 4) * 4 + 2 * colour + index // 4
-        targets = [(0, row, 2 * column + core)]
+        targets = [(1, column, 2 * row + where % 2, mirror.at[core, index % 4])]
         if g > 0:
-            targets.append((1, column, 2 * row + core))
-        for kind, to_grp, to_cell in targets:
+            for k in range(2):
+                targets.append((0, row, 2 * column + k, plain.at[where % 2, core, index % 4]))
+        for kind, to_grp, to_cell, dst in targets:
             here = jnp.logical_and(to_grp == grp, to_cell == cell)
-            src = piece.at[colour, g]
-            dst = mine.at[kind, where % 2, index % 4]
-            act(src, dst, kind, here, (to_grp, to_cell))
+            act(piece.at[colour, 2 * b + j], dst, kind, here, (to_grp, to_cell))
 
     def start_tile(src, dst, kind, here, target):
         @pl.when(here)
@@ -273,52 +278,52 @@
         def _():
             copy_to(src, dst, tile_send, tile_recv.at[kind], target).wait_send()
 
-    for colour in range(2):
-        here = y if colour == 0 else z
-        seven = crossed.at[colour, pl.ds(0, 7)]
-        copy_to(seven, seven, cross_send.at[colour], cross_recv.at[colour], peer).wait_recv()
-        acc = total[colour, here]
-        for d in range(1, 8):
-            acc = acc + crossed[colour, (here + d) % 8]
-        piece[colour] = acc
-        for g in range(3):
-            tile_copies(colour, g, start_tile)
-
-    apart = (cell // 8 - x) % 4
-    for kind in range(2):
-        used = apart != 3 if kind == 0 else apart >= 2
-
-        @pl.when(used)
-        def _(kind=kind):
-            whole = mine.at[kind]
-            copy_to(whole, whole, tile_send, tile_recv.at[kind], peer).wait_recv()
-
-        @pl.when(jnp.logical_not(used))
-        def _(kind=kind):
-            mine[kind] = jnp.zeros_like(mine[kind])
-
-    last = copy_to(mine, other, last_send, last_recv, peer)
-    last.start()
+    for b, groups in enumerate(BATCHES):
+        for colour in range(2):
+            here = y if colour == 0 else z
+            slots = pl.ds(2 * b, len(groups))
+            seven = crossed.at[colour, pl.ds(0, 7), slots]
+            copy_to(seven, seven, cross_send.at[b, colour], cross_recv.at[b, colour], peer).wait_recv()
+            acc = total[colour, here, slots]
+            for d in range(1, 8):
+                acc = acc + crossed[colour, (here + d) % 8, slots]
+            piece[colour, slots] = acc
+            for j in range(len(groups)):
+                tile_copies(colour, b, j, start_tile)
 
     for g in range(3):
         for colour in range(2):
             seven = part.at[g, core, colour, pl.ds(0, 7)]
             line_copy(g, colour, seven, seven, arrived_recv, peer).wait_send()
-            tile_copies(colour, g, finish_tile)
-    for colour in range(2):
-        seven = crossed.at[colour, pl.ds(0, 7)]
-        copy_to(seven, seven, cross_send.at[colour], cross_recv.at[colour], peer).wait_send()
-
-    last.wait()
-    first = core == 0
-    low = jnp.where(first, mine[...], other[...]).reshape(2, 2, 32, 128)
-    high = jnp.where(first, other[...], mine[...]).reshape(2, 2, 32, 128)
-
-    def whole_tile(kind):
-        return jnp.concatenate([low[kind, 0], high[kind, 0], low[kind, 1], high[kind, 1]], axis=0)
-
-    full = (whole_tile(0).T + whole_tile(1)) * (1.0 / CELLS)
-    out_ref[...] = jnp.where(first, full[:64], full[64:])
+    for b, groups in enumerate(BATCHES):
+        for colour in range(2):
+            seven = crossed.at[colour, pl.ds(0, 7), pl.ds(2 * b, len(groups))]
+            copy_to(seven, seven, cross_send.at[b, colour], cross_recv.at[b, colour], peer).wait_send()
+            for j in range(len(groups)):
+                tile_copies(colour, b, j, finish_tile)
+
+    apart = (cell // 8 - x) % 4
+    has_plain = jnp.logical_or(apart == 1, apart == 2)
+
+    @pl.when(jnp.logical_not(has_plain))
+    def _():
+        plain[...] = jnp.zeros_like(plain)
+
+    @pl.when(apart == 1)
+    def _():
+        mirror[...] = jnp.zeros_like(mirror)
+
+    @pl.when(has_plain)
+    def _():
+        copy_to(plain, plain, tile_send, tile_recv.at[0], peer).wait_recv()
+
+    @pl.when(apart != 1)
+    def _():
+        copy_to(mirror, mirror, tile_send, tile_recv.at[1], peer).wait_recv()
+
+    turned_back = plain[...].reshape(128, 128).T
+    columns = jnp.where(core == 0, turned_back[:64], turned_back[64:])
+    out_ref[...] = (columns + mirror[...].reshape(64, 128)) * (1.0 / CELLS)
 
 
 def body(snapshots, density):
@@ -343,9 +348,9 @@
             pltpu.VMEM((2, 8, 3, 8, 128), f32),
             pltpu.VMEM((2, 3, 8, 128), f32),
             pltpu.VMEM((2, 2, 4, 8, 128), f32),
-            pltpu.VMEM((2, 2, 4, 8, 128), f32),
+            pltpu.VMEM((2, 4, 8, 128), f32),
             dma, dma((CHUNKS, 4)), dma((CHUNKS, 4)), *[dma((CHUNKS,))] * 2, *[dma((HALF,))] * 4, dma((3,)), dma((3,)),
-            dma((3, 2)), dma((3, 2)), dma((3, 2)), dma((2,)), dma((2,)), dma, dma((2,)), dma, dma,
+            dma((3, 2)), dma((3, 2)), dma((3, 2)), dma((2, 2)), dma((2, 2)), dma, dma((2,)),
             pltpu.SemaphoreType.REGULAR, pltpu.SemaphoreType.REGULAR,
         ],
         compiler_params=pltpu.CompilerParams(

time: 69.4 us -> 66.9 us (0.964)
  the two profiles are of different devices: /device:TPU:61 before, /device:TPU:59 now
where the time goes in v5:
time: 66.9 us; the launch traced here: 66.7 us
  Pallas kernels  65.3 us (98%)
  local copies, waits for them, and re-layouts  1.38 us (2%)
    pallas_call x1, Pallas kernels, body(): pl.pallas_call(kernel, out_shape=jax.ShapeDtypeStruct((64, 128), f32), in...  65.3 us
    unnamed x1, local copies, waits for them, and re-layouts  1.38 us

profile of v5, /device:TPU:59, one launch (start us, length us, event | category | flops | bytes accessed | tf_op | source)
XLA Modules:
  0.0 66.7 jit_solution(580228196467442086)
XLA Ops:
  0.0 65.3 %shard_map.28 = f32[64,128]{1,0:T(8,128)} custom-call(bf16[3072,128]{1,0:T(8,128)(2,1)} %snap_hbm.1, f32[8]{0:T(128)} %density_ref.1), custom_call_target="tpu_custom_call" | custom-call | flops 1000000000 | bytes 1000000 | tf_op jit(solution)/shard_map/pallas_call | solution.py:331
  65.3 1.4 %copy.4 = f32[128,64]{0,1:T(8,128)} copy(f32[128,64]{0,1:T(8,128)} %bitcast.1) | data formatting | bytes 65536

commit v6 on v5

--- a/solution.py
+++ b/solution.py
@@ -13,6 +13,7 @@
 HALF = CHUNKS // 2
 AHEAD = 2
 EARLY = 4
+PIECED = 4
 BATCHES = ((0, 2), (1,))
 WIDE = QUARTER // CHUNKS
 SNAP = 128
@@ -91,6 +92,11 @@
     def x1_copy(c):
         return copy_to(own.at[c], next1.at[c], x1_send.at[c], x1_recv.at[c], device((x + 3) % 4, y, z, core))
 
+    def x1_piece(c, q):
+        return copy_to(
+            own.at[c, q], next1.at[c, q], x1_send.at[c], x1_recv.at[c], device((x + 3) % 4, y, z, core)
+        )
+
     def pass_copy(n):
         return copy_to(
             own.at[chunk(n)], passing.at[n], pass_send.at[n], pass_recv.at[n], device((x + 1) % 4, y, z, core)
@@ -112,44 +118,77 @@
             weigh(chunk(n))
         if n < AHEAD:
             start_y(n)
+        if n >= PIECED:
+            x1_piece(chunk(n), ylo).start()
 
     for d in range(1, 8):
         greet(plane_sem, d, "y")
+
+    def multiply(g, colour, pairs, more=False):
+        left = jnp.concatenate([pair[0] for pair in pairs], axis=-1).reshape(512, len(pairs) * WIDE)
+        right = jnp.concatenate([pair[1] for pair in pairs], axis=-1).reshape(256, len(pairs) * WIDE)
+        product = lax.dot_general(left, right, (((1,), (1,)), ((), ())), preferred_element_type=jnp.float32)
+        for n in range(8):
+            for h in range(2):
+                for t in range(2):
+                    term = product[n * 64 + h * 32 : n * 64 + h * 32 + 32, t * 128 : t * 128 + 128]
+                    if more:
+                        term = term + part[g, h, colour, n, t]
+                    part[g, h, colour, n, t] = term
+
+    def core_copy(g, colour):
+        return copy_to(
+            part.at[g, 1 - core, colour], peer_part.at[g, colour],
+            core_send.at[g, colour], core_recv.at[g, colour], peer,
+        )
+
+    def columns_of(colour):
+        return slice(2 * colour, 2 * colour + 2)
+
+    def multiply0(first, last, more):
+        for colour in range(2):
+            multiply(
+                0, colour, [(own[chunk(n)], own[chunk(n), columns_of(colour)]) for n in range(first, last)], more
+            )
+            if more:
+                core_copy(0, colour).start()
+
+    def multiply1(first, last, more):
+        for colour in range(2):
+            multiply(
+                1, colour, [(own[chunk(n)], next1[chunk(n), columns_of(colour)]) for n in range(first, last)], more
+            )
+            if more:
+                core_copy(1, colour).start()
+
+    def multiply2():
+        for colour in range(2):
+            multiply(2, colour, [(own[half * HALF + n], next2[n, columns_of(colour)]) for n in range(HALF)])
+            core_copy(2, colour).start()
 
     for n in range(CHUNKS):
         for d in (1, 2, 3):
             y_arrival(chunk(n), other_y(d)).wait_recv()
+            if n >= PIECED:
+                x1_piece(chunk(n), other_y(d)).start()
         if n + AHEAD < CHUNKS:
             for d in (1, 2, 3):
                 y_copy(chunk(n), other_y(d)).wait_send()
             start_y(n + AHEAD)
-        x1_copy(chunk(n)).start()
+        if n < PIECED:
+            x1_copy(chunk(n)).start()
         if n < HALF:
             pass_copy(n).start()
         if 2 <= n < HALF + 2:
             pass_copy(n - 2).wait_recv()
             x2_copy(n - 2).start()
+        if n == EARLY:
+            multiply0(0, EARLY, False)
 
     pl.semaphore_wait(plane_sem, 7)
     for d in range(1, 4):
         greet(all_sem, d, "x")
 
-    def multiply(g, pairs, more=False):
-        left, right = (
-            jnp.concatenate([pair[k] for pair in pairs], axis=-1).reshape(512, len(pairs) * WIDE) for k in (0, 1)
-        )
-        product = lax.dot_general(left, right, (((1,), (1,)), ((), ())), preferred_element_type=jnp.float32)
-        for n in range(8):
-            for h in range(2):
-                for t in range(4):
-                    term = product[n * 64 + h * 32 : n * 64 + h * 32 + 32, t * 128 : t * 128 + 128]
-                    if more:
-                        term = term + part[g, h, t // 2, n, t % 2]
-                    part[g, h, t // 2, n, t % 2] = term
-
-    def core_copy(g):
-        return copy_to(part.at[g, 1 - core], peer_part.at[g], core_send.at[g], core_recv.at[g], peer)
-
     def place(colour):
         return z if colour == 0 else y
 
@@ -161,14 +200,14 @@
         return copy_to(src, dst, line_send.at[g, colour], recv.at[g, colour], target)
 
     def spread(g):
-        core_copy(g).wait_recv()
-        part[g, core] = part[g, core] + peer_part[g]
-        for colour in range(2):
+        for colour in range(2):
+            core_copy(g, colour).wait_recv()
+            part[g, core, colour] = part[g, core, colour] + peer_part[g, colour]
             terms = part.at[g, core, colour]
             for s, way in ((0, 1), (1, -1)):
-                beside, target = at_line(colour, way)
                 third, _ = at_line(colour, 3 * way)
                 fourth, _ = at_line(colour, 4)
+                _, target = at_line(colour, way)
                 _, target2 = at_line(colour, 2 * way)
                 slot = between.at[g, colour, s]
                 line_copy(g, colour, terms.at[third], slot.at[pl.ds(0, 2)], between_recv, target).start()
@@ -190,23 +229,18 @@
                 terms[there, s] = terms[there, s] + between[g, colour, s, 2]
                 line_copy(g, colour, terms.at[there], arrived.at[g, colour, 2 + s], arrived_recv, target).start()
 
-    multiply(0, [(own[c], own[c]) for c in range(CHUNKS)])
-    core_copy(0).start()
-
+    multiply0(EARLY, CHUNKS, True)
     for n in range(HALF):
         x2_copy(n).wait_recv()
-    multiply(2, [(own[half * HALF + n], next2[n]) for n in range(HALF)])
-    core_copy(2).start()
+    multiply2()
     spread(0)
-
     for n in range(EARLY):
         x1_copy(chunk(n)).wait_recv()
-    multiply(1, [(own[chunk(n)], next1[chunk(n)]) for n in range(EARLY)])
+    multiply1(0, EARLY, False)
     spread(2)
     for n in range(EARLY, CHUNKS):
         x1_copy(chunk(n)).wait_recv()
-    multiply(1, [(own[chunk(n)], next1[chunk(n)]) for n in range(EARLY, CHUNKS)], more=True)
-    core_copy(1).start()
+    multiply1(EARLY, CHUNKS, True)
     spread(1)
     send_on(0)
     send_on(2)
@@ -235,7 +269,8 @@
             pass_copy(n).wait_send()
             x2_copy(n).wait_send()
     for g in range(3):
-        core_copy(g).wait_send()
+        for colour in range(2):
+            core_copy(g, colour).wait_send()
 
     for b, groups in enumerate(BATCHES):
         for colour in range(2):
@@ -323,7 +358,7 @@
 
     turned_back = plain[...].reshape(128, 128).T
     columns = jnp.where(core == 0, turned_back[:64], turned_back[64:])
-    out_ref[...] = (columns + mirror[...].reshape(64, 128)) * (1.0 / CELLS)
+    out_ref[...] = columns + mirror[...].reshape(64, 128)
 
 
 def body(snapshots, density):
@@ -349,15 +384,15 @@
             pltpu.VMEM((2, 3, 8, 128), f32),
             pltpu.VMEM((2, 2, 4, 8, 128), f32),
             pltpu.VMEM((2, 4, 8, 128), f32),
-            dma, dma((CHUNKS, 4)), dma((CHUNKS, 4)), *[dma((CHUNKS,))] * 2, *[dma((HALF,))] * 4, dma((3,)), dma((3,)),
+            dma, dma((CHUNKS, 4)), dma((CHUNKS, 4)), *[dma((CHUNKS,))] * 2, *[dma((HALF,))] * 4, dma((3, 2)), dma((3, 2)),
             dma((3, 2)), dma((3, 2)), dma((3, 2)), dma((2, 2)), dma((2, 2)), dma, dma((2,)),
             pltpu.SemaphoreType.REGULAR, pltpu.SemaphoreType.REGULAR,
         ],
         compiler_params=pltpu.CompilerParams(
-            collective_id=0, has_side_effects=True, vmem_limit_bytes=60 * 2**20
+            collective_id=0, has_side_effects=True, vmem_limit_bytes=55000 * 1024
         ),
         cost_estimate=pl.CostEstimate(flops=10**9, bytes_accessed=10**6, transcendentals=0),
-    )(snapshots, density).T
+    )(snapshots, density).T * (1.0 / CELLS)
 
 
 def solution(mesh):

time: 66.9 us -> 66.1 us (0.988)
  local copies, waits for them, and re-layouts: 1.38 us -> 0.65 us
    unnamed x1 -> x2, local copies, waits for them, and re-layouts: 1.38 us -> 0.65 us
where the time goes in v6:
time: 66.1 us; the launch traced here: 66 us
  Pallas kernels  64.7 us (98%)
    pallas_call x1, Pallas kernels, body(): pl.pallas_call(kernel, out_shape=jax.ShapeDtypeStruct((64, 128), f32), in...  64.7 us

profile of v6, /device:TPU:59, one launch (start us, length us, event | category | flops | bytes accessed | tf_op | source)
XLA Modules:
  0.0 66.0 jit_solution(1283181155066823197)
XLA Ops:
  0.0 0.0 copy-start
  0.0 0.7 copy-done
  0.7 64.7 %shard_map.28 = f32[64,128]{1,0:T(8,128)S(1)} custom-call(bf16[3072,128]{1,0:T(8,128)(2,1)} %snap_hbm.1, f32[8]{0:T(128)S(1)} %copy-done), custom_call_target="tpu_custom_call" | custom-call | flops 1000000000 | bytes 1000000 | tf_op jit(solution)/shard_map/pallas_call | solution.py:366
  65.4 0.6 multiply_bitcast_fusion
Async XLA Ops:
  0.0 0.7 copy-start

commit v7 on v6

--- a/solution.py
+++ b/solution.py
@@ -41,8 +41,17 @@
     y_base = y - ylo
     peer = (grp, cell + 1 - 2 * core)
 
-    load = pltpu.make_async_copy(snap_hbm, snap, load_sem)
-    load.start()
+    half = x // 2
+    first_chunk = (1 - half) * HALF
+
+    def chunk(n):
+        return (n + first_chunk) % CHUNKS
+
+    def load(c):
+        return pltpu.make_async_copy(snap_hbm.at[:, c], snap.at[:, c], load_sem.at[c])
+
+    for n in range(CHUNKS):
+        load(chunk(n)).start()
 
     barrier = pltpu.get_barrier_semaphore()
 
@@ -61,19 +70,12 @@
         greet(barrier, d, "z")
     pl.semaphore_signal(barrier, inc=1, device_id=peer, device_id_type=MESH)
 
-    half = x // 2
-    first_chunk = (1 - half) * HALF
-
-    def chunk(n):
-        return (n + first_chunk) % CHUNKS
-
-    load.wait()
     scale = jnp.sqrt(jnp.full((1, SNAP), density_ref[z], jnp.float32))
 
     def weigh(c):
+        load(c).wait()
         for q in range(4):
-            rows = pl.ds(pl.multiple_of(q * QUARTER + c * WIDE, WIDE), WIDE)
-            turned[q, c] = (snap[rows, :].astype(jnp.float32) * scale).astype(jnp.bfloat16).T
+            turned[q, c] = (snap[q, c].astype(jnp.float32) * scale).astype(jnp.bfloat16).T
         own[c, ylo] = turned[ylo, c]
 
     def other_y(d):
@@ -369,7 +371,7 @@
         in_specs=[pl.BlockSpec(memory_space=pl.ANY), pl.BlockSpec(memory_space=pltpu.SMEM)],
         out_specs=pl.BlockSpec(memory_space=pltpu.VMEM),
         scratch_shapes=[
-            pltpu.VMEM((SLAB, SNAP), bf16),
+            pltpu.VMEM((4, CHUNKS, WIDE, SNAP), bf16),
             pltpu.VMEM((4, CHUNKS, SNAP, WIDE), bf16),
             pltpu.VMEM((CHUNKS, 4, SNAP, WIDE), bf16),
             pltpu.VMEM((CHUNKS, 4, SNAP, WIDE), bf16),
@@ -384,7 +386,7 @@
             pltpu.VMEM((2, 3, 8, 128), f32),
             pltpu.VMEM((2, 2, 4, 8, 128), f32),
             pltpu.VMEM((2, 4, 8, 128), f32),
-            dma, dma((CHUNKS, 4)), dma((CHUNKS, 4)), *[dma((CHUNKS,))] * 2, *[dma((HALF,))] * 4, dma((3, 2)), dma((3, 2)),
+            dma((CHUNKS,)), dma((CHUNKS, 4)), dma((CHUNKS, 4)), *[dma((CHUNKS,))] * 2, *[dma((HALF,))] * 4, dma((3, 2)), dma((3, 2)),
             dma((3, 2)), dma((3, 2)), dma((3, 2)), dma((2, 2)), dma((2, 2)), dma, dma((2,)),
             pltpu.SemaphoreType.REGULAR, pltpu.SemaphoreType.REGULAR,
         ],
@@ -392,7 +394,7 @@
             collective_id=0, has_side_effects=True, vmem_limit_bytes=55000 * 1024
         ),
         cost_estimate=pl.CostEstimate(flops=10**9, bytes_accessed=10**6, transcendentals=0),
-    )(snapshots, density).T * (1.0 / CELLS)
+    )(snapshots.reshape(4, CHUNKS, WIDE, SNAP), density).T * (1.0 / CELLS)
 
 
 def solution(mesh):

time: 66.1 us -> 66.2 us (level)
  no operation moved by 1% of the time
where the time goes in v7:
time: 66.2 us; the launch traced here: 66.1 us
  Pallas kernels  64.8 us (98%)
    pallas_call x1, Pallas kernels, body(): pl.pallas_call(kernel, out_shape=jax.ShapeDtypeStruct((64, 128), f32), in...  64.8 us

profile of v7, /device:TPU:59, one launch (start us, length us, event | category | flops | bytes accessed | tf_op | source)
XLA Modules:
  0.0 66.1 jit_solution(14507621809369363614)
XLA Ops:
  0.0 0.0 copy-start
  0.0 0.7 copy-done
  0.7 64.8 %shard_map.28 = f32[64,128]{1,0:T(8,128)S(1)} custom-call(bf16[4,6,128,128]{3,2,1,0:T(8,128)(2,1)} %bitcast.3, f32[8]{0:T(128)S(1)} %copy-done), custom_call_target="tpu_custom_call" | custom-call | flops 1000000000 | bytes 1000000 | tf_op jit(solution)/shard_map/pallas_call | solution.py:368
  65.5 0.6 multiply_bitcast_fusion
Async XLA Ops:
  0.0 0.7 copy-start

commit v8 on v6

--- a/solution.py
+++ b/solution.py
@@ -192,9 +192,17 @@
     def place(colour):
         return z if colour == 0 else y
 
+    line_shift = (2 * x + 5, 5)
+    rows_here = ((z + 16 - line_shift[0]) % 8, (y + 16 - line_shift[1]) % 8)
+    cross_shift = (4 * (rows_here[0] // 2) + 5, 7 * (rows_here[1] // 2) + 2 * x + 7)
+
+    def part_of(colour, there):
+        return (there + 40 - cross_shift[colour]) % 8
+
     def at_line(colour, d):
         there = (place(colour) + d + 8) % 8
-        return there, device(x, y, there, core) if colour == 0 else device(x, there, z, core)
+        rows = (there + 16 - line_shift[colour]) % 8
+        return rows, device(x, y, there, core) if colour == 0 else device(x, there, z, core)
 
     def line_copy(g, colour, src, dst, recv, target):
         return copy_to(src, dst, line_send.at[g, colour], recv.at[g, colour], target)
@@ -256,7 +264,7 @@
             target = device(x, y, there, core)
         groups = pl.ds(2 * b, len(BATCHES[b]))
         return copy_to(
-            total.at[colour, there, groups], crossed.at[colour, here, groups],
+            total.at[colour, part_of(colour, there), groups], crossed.at[colour, here, groups],
             cross_send.at[b, colour], cross_recv.at[b, colour], target,
         )
 
@@ -277,7 +285,7 @@
             for j, g in enumerate(groups):
                 whole = arrived.at[g, colour]
                 line_copy(g, colour, whole, whole, arrived_recv, peer).wait_recv()
-                acc = part[g, core, colour, place(colour)]
+                acc = part[g, core, colour, rows_here[colour]]
                 for d in range(4):
                     acc = acc + arrived[g, colour, d]
                 total[colour, :, 2 * b + j] = acc.reshape(8, 8, 128)
@@ -288,7 +296,7 @@
 
     def tile_copies(colour, b, j, act):
         g = BATCHES[b][j]
-        where, index = (z, y) if colour == 0 else (y, z)
+        where, index = rows_here[colour], part_of(colour, y if colour == 0 else z)
         row = x * 4 + where // 2
         column = ((x + g) % 4) * 4 + 2 * colour + index // 4
         targets = [(1, column, 2 * row + where % 2, mirror.at[core, index % 4])]
@@ -319,7 +327,7 @@
             slots = pl.ds(2 * b, len(groups))
             seven = crossed.at[colour, pl.ds(0, 7), slots]
             copy_to(seven, seven, cross_send.at[b, colour], cross_recv.at[b, colour], peer).wait_recv()
-            acc = total[colour, here, slots]
+            acc = total[colour, part_of(colour, here), slots]
             for d in range(1, 8):
                 acc = acc + crossed[colour, (here + d) % 8, slots]
             piece[colour, slots] = acc

time: 66.1 us -> 66.3 us (level)
  the two profiles are of different devices: /device:TPU:59 before, /device:TPU:2 now
where the time goes in v8:
time: 66.3 us; the launch traced here: 66.1 us
  Pallas kernels  64.8 us (98%)
    pallas_call x1, Pallas kernels, body(): pl.pallas_call(kernel, out_shape=jax.ShapeDtypeStruct((64, 128), f32), in...  64.8 us

profile of v8, /device:TPU:2, one launch (start us, length us, event | category | flops | bytes accessed | tf_op | source)
XLA Modules:
  0.0 66.1 jit_solution(17462497158102339102)
XLA Ops:
  0.0 0.0 copy-start
  0.0 0.7 copy-done
  0.7 64.8 %shard_map.28 = f32[64,128]{1,0:T(8,128)S(1)} custom-call(bf16[3072,128]{1,0:T(8,128)(2,1)} %snap_hbm.1, f32[8]{0:T(128)S(1)} %copy-done), custom_call_target="tpu_custom_call" | custom-call | flops 1000000000 | bytes 1000000 | tf_op jit(solution)/shard_map/pallas_call | solution.py:374
  65.5 0.6 multiply_bitcast_fusion
Async XLA Ops:
  0.0 0.7 copy-start
